TPU v7x, 256 devices: a whole 4x4x8 slice. The times are simulated.
256 devices in a mesh: dp: 16 (over z_hi, x, core), tensor: 16 (over z_lo, y).
Axes of the slice: x: 4, y: 4, z: 8 (z_hi: 2, z_lo: 4; z = z_hi * 4 + z_lo), core: 2. Of those that a mesh axis runs over, the one named last changes fastest.
Arguments:
- inputs: bfloat16 [6144, 2560], P(('dp', 'tensor')), may hold values from -6 to 6
- norm_gain: float32 [2560], replicated, may hold values from 0.5 to 1.5
- w_up: bfloat16 [2560, 10240], P(None, 'tensor'), may hold values from -0.07905694 to 0.07905694
- w_down: bfloat16 [10240, 2560], P('tensor'), may hold values from -0.0625 to 0.0625
- grad_out: bfloat16 [6144, 2560], P(('dp', 'tensor')), may hold values from -7 to 7
Outputs:
- output: bfloat16 [6144, 2560], P(('dp', 'tensor'))
- grad_in: bfloat16 [6144, 2560], P(('dp', 'tensor'))
- grad_up: bfloat16 [2560, 10240], P(None, 'tensor')
- grad_down: bfloat16 [10240, 2560], P('tensor')
- grad_gain: float32 [2560], replicated
All inputs are finite; a program needn't handle non-finite values.
Results may differ from a plain program's by a relative error of at most 0.024.
Values may be sent and summed in bfloat16 or wider, within the bound.
A program may use at most 192 MiB of HBM per device.

v0:
```python
import math
import jax
import jax.numpy as jnp
from jax import lax
from jax.sharding import PartitionSpec as P

BLOCK = 16
TWO_PI = 2.0 * math.pi
CONTRACT_ROWS = (((0,), (0,)), ((), ()))
CONTRACT_COLS = (((1,), (1,)), ((), ()))


def staircase(values):
    return values - jnp.sin(TWO_PI * values) / TWO_PI


def block_peak(values):
    row_count, col_count = values.shape
    block_max = jnp.max(jnp.abs(values).reshape(row_count, col_count // BLOCK, BLOCK), axis=2)
    return jnp.repeat(block_max, BLOCK, axis=1)


def per_device(inputs, norm_gain, w_up, w_down, grad_out):
    widened = inputs.astype(jnp.float32)
    inverse = lax.rsqrt(jnp.mean(widened * widened, axis=1, keepdims=True) + 1e-05)
    normed = widened * inverse * norm_gain
    x_scale = jnp.maximum(block_peak(normed), 1.5) / 6.0
    quantized = (x_scale * staircase(normed / x_scale)).astype(jnp.bfloat16)
    gathered = lax.all_gather(quantized, "tensor", axis=0, tiled=True)
    pre_act = jnp.dot(gathered, w_up, preferred_element_type=jnp.float32)
    active = jnp.maximum(pre_act, 0.0)
    hidden = active * active
    peak_value = lax.pmax(jnp.max(hidden), "tensor") + 1e-06
    h_scale = jnp.maximum(block_peak(hidden), peak_value / 8.0) / 6.0
    hidden_q = (h_scale * staircase(hidden / h_scale)).astype(jnp.bfloat16)
    picked = hidden_q
    output = lax.psum_scatter(
        jnp.dot(picked, w_down, preferred_element_type=jnp.float32).astype(jnp.bfloat16),
        "tensor",
        scatter_dimension=0,
        tiled=True,
    )
    cotangent = lax.all_gather(grad_out, "tensor", axis=0, tiled=True)
    down_part = lax.dot_general(
        hidden_q, cotangent, CONTRACT_ROWS, preferred_element_type=jnp.float32
    )
    down_sum = None
    grad_hq = lax.dot_general(cotangent, w_down, CONTRACT_COLS, preferred_element_type=jnp.float32)
    grad_z = (grad_hq * 2.0 * active).astype(jnp.bfloat16)
    picked = grad_z
    grad_xq = lax.psum_scatter(
        lax.dot_general(picked, w_up, CONTRACT_COLS, preferred_element_type=jnp.float32).astype(
            jnp.bfloat16
        ),
        "tensor",
        scatter_dimension=0,
        tiled=True,
    ).astype(jnp.float32)
    grad_gain = lax.psum(jnp.sum(grad_xq * widened * inverse, axis=0), ("dp", "tensor"))
    scaled = grad_xq * norm_gain
    cubed = inverse * inverse * inverse
    grad_in = (
        inverse * scaled - widened * cubed * jnp.mean(scaled * widened, axis=1, keepdims=True)
    ).astype(jnp.bfloat16)
    up_part = lax.dot_general(gathered, grad_z, CONTRACT_ROWS, preferred_element_type=jnp.float32)
    up_sum, down_sum = (
        lax.psum(up_part.astype(jnp.bfloat16), "dp").astype(jnp.float32),
        lax.psum(down_part.astype(jnp.bfloat16), "dp").astype(jnp.float32),
    )
    return (output, grad_in, up_sum.astype(jnp.bfloat16), down_sum.astype(jnp.bfloat16), grad_gain)


def solution(mesh):
    return jax.shard_map(
        per_device,
        mesh=mesh,
        in_specs=(
            P(("dp", "tensor"), None),
            P(),
            P(None, "tensor"),
            P("tensor", None),
            P(("dp", "tensor"), None),
        ),
        out_specs=(
            P(("dp", "tensor"), None),
            P(("dp", "tensor"), None),
            P(None, "tensor"),
            P("tensor", None),
            P(),
        ),
        check_vma=False,
    )
```

profile of v0, /device:TPU:8, one launch (start us, length us, event | category | flops | bytes accessed | tf_op | source)
XLA Modules:
  0.0 601.0 jit_solution(18340379943486654333)
XLA Ops:
  9.4 1.9 reshape.45
  11.4 2.5 reduce_max.27
  13.9 1.8 broadcast_in_dim.4
  15.7 3.6 div.40
  19.4 2.5 multiply_convert_fusion.1
  22.7 85.2 %all-gather.3.cloned.1.call-done = bf16[384,2560]{1,0:T(8,128)(2,1)} async-done(((bf16[24,2560]{1,0:T(8,128)(2,1)}), bf16[384,2560]{1,0:T(8,128)(2,1)}) %all-gather.3.cloned.1.call-update) | async-done | bytes 1966096 | tf_op jit(solution)/shard_map/all_gather | solution.py:29
  107.9 5.1 multiply_reduce_fusion
  113.0 78.2 %all-gather.5.cloned.1.call-done = bf16[384,2560]{1,0:T(8,128)(2,1)} async-done(((bf16[24,2560]{1,0:T(8,128)(2,1)}), bf16[384,2560]{1,0:T(8,128)(2,1)}) %all-gather.5.cloned.1.call-update) | async-done | bytes 1966096 | tf_op jit(solution)/shard_map/all_gather | solution.py:43
  191.3 4.5 fusion.1
  196.5 3.0 convolution_convert_fusion.2
  199.6 39.0 %pmax.7 = f32[]{:T(128)} all-reduce(f32[]{:T(128)} %get-tuple-element.9), channel_id=1, replica_groups=mesh['dp'=16,'tensor'=16] {'tensor'}, use_global_device_ids=true, to_apply=%region_4.0 | all-reduce | flops 1 | bytes 8 | tf_op jit(solution)/shard_map/pmax | solution.py:33
  238.7 2.5 copy.10
  244.2 2.5 copy.12
  246.7 4.6 multiply_convert_fusion
  252.1 5.0 convolution_convert_fusion.3
  257.3 5.6 convolution_convert_fusion.1
  262.9 3.6 convolution_convert_fusion
  266.5 14.8 %reduce-scatter.5.cloned.1.call-done = bf16[24,2560]{1,0:T(8,128)(2,1)} async-done(((bf16[384,2560]{1,0:T(8,128)(2,1)}), bf16[24,2560]{1,0:T(8,128)(2,1)}) %reduce-scatter.5.cloned.1.call-update) | async-done | bytes 122896 | tf_op jit(solution)/shard_map/reduce_scatter | solution.py:51
  282.4 78.7 %psum.23 = f32[2560]{0:T(1024)} all-reduce(f32[2560]{0:T(1024)S(1)} %get-tuple-element.5), channel_id=1, replica_groups=mesh['dp'=16,'tensor'=16] {'dp','tensor'}, use_global_device_ids=true, to_apply=%region_11.0 | all-reduce | flops 2560 | bytes 20480 | tf_op jit(solution)/shard_map/psum | solution.py:59
  361.1 1.7 fusion.4
  362.8 5.7 reduce-scatter.3.cloned.1.call-done
  368.5 220.3 %all-reduce.3.cloned.1.call-done = (bf16[2560,640]{1,0:T(8,128)(2,1)}, bf16[640,2560]{1,0:T(8,128)(2,1)}) async-done(((bf16[2560,640]{1,0:T(8,128)(2,1)}, bf16[640,2560]{1,0:T(8,128)(2,1)}), (bf16[2560,640]{1,0:T(8,128)(2,1)}, bf16[640,2560]{1,0:T(8,128)(2,1)})) %all-reduce.3.cloned.1.call-update) | async-done | bytes 6553616 | tf_op jit(solution)/shard_map/psum | solution.py:67
  588.7 4.1 copy.15
  592.8 1.7 copy.16
  (35 shorter events, 8.5 us)
Async XLA Ops:
  7.2 100.8 %copy-start = (bf16[2560,640]{1,0:T(8,128)(2,1)S(1)}, bf16[2560,640]{1,0:T(8,128)(2,1)}, u32[]{:S(2)}) copy-start(bf16[2560,640]{1,0:T(8,128)(2,1)} %param.7) | copy-start | bytes 9830404
  7.2 100.8 %all-gather.3.cloned.1.call-start = ((), (), s32[]{:S(2)}) async-start(), calls=%async_computation.2 | async-start | bytes 2088960 | tf_op jit(solution)/shard_map/all_gather | solution.py:29
  11.4 8.0 %copy-start.2 = (bf16[24,2560]{1,0:T(8,128)(2,1)S(1)}, bf16[24,2560]{1,0:T(8,128)(2,1)}, u32[]{:S(2)}) copy-start(bf16[24,2560]{1,0:T(8,128)(2,1)} %param.5) | copy-start | bytes 368644
  11.4 8.0 %copy-start.5 = (f32[2560]{0:T(1024)S(1)}, f32[2560]{0:T(1024)}, u32[]{:S(2)}) copy-start(f32[2560]{0:T(1024)} %param.6) | copy-start | bytes 30724
  21.9 169.4 %all-gather.5.cloned.1.call-start = ((), (), s32[]{:S(2)}) async-start(), calls=%async_computation.4 | async-start | bytes 2088960 | tf_op jit(solution)/shard_map/all_gather | solution.py:43
  22.7 258.6 %reduce-scatter.5.cloned.1.call-start = ((), (), s32[]{:S(2)}) async-start(), calls=%async_computation.5 | async-start | bytes 2088960 | tf_op jit(solution)/shard_map/reduce_scatter | solution.py:51
  195.8 0.8 copy-start.7
  199.6 168.9 %reduce-scatter.3.cloned.1.call-start = ((), (), s32[]{:S(2)}) async-start(), calls=%async_computation.3 | async-start | bytes 2088960 | tf_op jit(solution)/shard_map/reduce_scatter | solution.py:37
  251.3 0.8 copy-start.3
  257.0 331.7 %all-reduce.3.cloned.1.call-start = ((), (), s32[]{:S(2)}) async-start(), calls=%async_computation.6 | async-start | bytes 13107200 | tf_op jit(solution)/shard_map/psum | solution.py:67
  257.3 5.6 copy-start.4
  257.3 5.6 copy-start.6
  588.7 4.1 copy-start.1
Sparse Core Ops, SparseCore 0:
  22.0 85.8 all-gather.2
  109.7 81.4 all-gather.4
  199.7 81.5 reduce-scatter.4
  284.4 83.9 reduce-scatter.2
  371.6 217.0 all-reduce.2
where the time goes:
time: 602 us; the launch traced here: 601 us
  waiting for transfers between devices  405 us (67%)
  blocking collectives  118 us (20%)
  matrix products  26.8 us (4%)
  local copies, waits for them, and re-layouts  20.8 us (3%)
  other arithmetic  15.9 us (3%)
  between operations  14.5 us (2%)
    psum x1, waiting for transfers between devices, per_device(): lax.psum(up_part.astype(jnp.bfloat16), 'dp').astype(jnp.float32)  220 us
    all_gather x1, waiting for transfers between devices, per_device(): gathered = lax.all_gather(quantized, 'tensor', axis=0, tiled=True)  85.2 us
    psum x1, blocking collectives, per_device(): lax.psum(jnp.sum(grad_xq * widened * inverse, axis=0), ('dp', 'tensor'))  78.7 us
    all_gather x1, waiting for transfers between devices, per_device(): cotangent = lax.all_gather(grad_out, 'tensor', axis=0, tiled=True)  78.2 us
    pmax x1, blocking collectives, per_device(): peak_value = lax.pmax(jnp.max(hidden), 'tensor') + 1e-06  39 us
    reduce_scatter x1, waiting for transfers between devices, per_device(): lax.psum_scatter(lax.dot_general(picked, w_up, CONTRACT_COLS, preferred_e...  14.8 us
  transfers between devices with their start and end apart: 5, of which 5 were waited for; matrix products, arithmetic and copies ran while one was open for 6% of the time, Pallas kernels for 0%

commit v1 on v0

--- a/solution.py
+++ b/solution.py
@@ -64,7 +64,7 @@
     ).astype(jnp.bfloat16)
     up_part = lax.dot_general(gathered, grad_z, CONTRACT_ROWS, preferred_element_type=jnp.float32)
     up_sum, down_sum = (
-        lax.psum(up_part.astype(jnp.bfloat16), "dp").astype(jnp.float32),
+        jnp.sum(lax.all_gather(up_part.astype(jnp.bfloat16), "dp"), axis=0).astype(jnp.float32),
         lax.psum(down_part.astype(jnp.bfloat16), "dp").astype(jnp.float32),
     )
     return (output, grad_in, up_sum.astype(jnp.bfloat16), down_sum.astype(jnp.bfloat16), grad_gain)

time: 602 us -> 1030 us (1.71)
  waiting for transfers between devices: 405 us -> 770 us
  blocking collectives: 118 us -> 171 us
  other arithmetic: 15.9 us -> 33.5 us
    all_gather x0 -> x1, waiting for transfers between devices: none -> 331 us  [per_device(): lax.all_gather(up_part.astype(jnp.bfloat16), 'dp')]
    reduce_scatter x1, waiting for transfers between devices: 5.7 us -> 86.6 us  [per_device(): lax.psum_scatter(jnp.dot(picked, w_down, preferred_element_type=jnp.float...]
    psum x1, waiting for transfers between devices: 220 us -> 166 us  [per_device(): lax.psum(down_part.astype(jnp.bfloat16), 'dp').astype(jnp.float32)]
    psum x1, blocking collectives: 78.7 us -> 131 us  [per_device(): lax.psum(jnp.sum(grad_xq * widened * inverse, axis=0), ('dp', 'tensor'))]
    reduce_sum x0 -> x1, other arithmetic: none -> 19.8 us  [per_device(): jnp.sum(lax.all_gather(up_part.astype(jnp.bfloat16), 'dp'), axis=0)]
  transfers between devices with their start and end apart: 5 -> 6, of which waited for: 5 -> 6; matrix products, arithmetic and copies ran while one was open for 6% -> 5% of each run, Pallas kernels for 0% -> 0%
where the time goes in v1:
time: 1030 us
  waiting for transfers between devices  770 us (75%)
  blocking collectives  171 us (17%)
  other arithmetic  33.5 us (3%)
  matrix products  28 us (3%)
  between operations  14.9 us (1%)
  local copies, waits for them, and re-layouts  12.8 us (1%)
    all_gather x1, waiting for transfers between devices, per_device(): lax.all_gather(up_part.astype(jnp.bfloat16), 'dp')  331 us
    psum x1, waiting for transfers between devices, per_device(): lax.psum(down_part.astype(jnp.bfloat16), 'dp').astype(jnp.float32)  166 us
    psum x1, blocking collectives, per_device(): lax.psum(jnp.sum(grad_xq * widened * inverse, axis=0), ('dp', 'tensor'))  131 us
    reduce_scatter x1, waiting for transfers between devices, per_device(): lax.psum_scatter(jnp.dot(picked, w_down, preferred_element_type=jnp.float...  86.6 us
    all_gather x1, waiting for transfers between devices, per_device(): gathered = lax.all_gather(quantized, 'tensor', axis=0, tiled=True)  85.2 us
    all_gather x1, waiting for transfers between devices, per_device(): cotangent = lax.all_gather(grad_out, 'tensor', axis=0, tiled=True)  78.2 us
    pmax x1, blocking collectives, per_device(): peak_value = lax.pmax(jnp.max(hidden), 'tensor') + 1e-06  39.2 us
    reduce_scatter x1, waiting for transfers between devices, per_device(): lax.psum_scatter(lax.dot_general(picked, w_up, CONTRACT_COLS, preferred_e...  21.8 us
  transfers between devices with their start and end apart: 6, of which 6 were waited for; matrix products, arithmetic and copies ran while one was open for 5% of the time, Pallas kernels for 0%

profile of v1, /device:TPU:8, one launch (start us, length us, event | category | flops | bytes accessed | tf_op | source)
XLA Modules:
  0.0 1029.7 jit_solution(13394829930385833689)
XLA Ops:
  7.2 1.2 fusion.5
  9.4 1.9 reshape.45
  11.4 2.5 reduce_max.27
  13.9 1.8 broadcast_in_dim.4
  15.7 3.6 div.40
  19.4 2.5 multiply_convert_fusion.1
  22.7 85.2 %all-gather.5.cloned.1.call-done = bf16[384,2560]{1,0:T(8,128)(2,1)} async-done(((bf16[24,2560]{1,0:T(8,128)(2,1)}), bf16[384,2560]{1,0:T(8,128)(2,1)}) %all-gather.5.cloned.1.call-update) | async-done | bytes 1966096 | tf_op jit(solution)/shard_map/all_gather | solution.py:29
  107.9 5.1 multiply_reduce_fusion
  113.0 78.2 %all-gather.7.cloned.1.call-done = bf16[384,2560]{1,0:T(8,128)(2,1)} async-done(((bf16[24,2560]{1,0:T(8,128)(2,1)}), bf16[384,2560]{1,0:T(8,128)(2,1)}) %all-gather.7.cloned.1.call-update) | async-done | bytes 1966096 | tf_op jit(solution)/shard_map/all_gather | solution.py:43
  191.3 4.5 fusion.1
  196.6 3.0 convolution_convert_fusion.2
  199.6 5.4 convolution_convert_fusion.1
  205.1 39.2 %pmax.7 = f32[]{:T(128)} all-reduce(f32[]{:T(128)} %get-tuple-element.7), channel_id=1, replica_groups=mesh['dp'=16,'tensor'=16] {'tensor'}, use_global_device_ids=true, to_apply=%region_4.0 | all-reduce | flops 1 | bytes 8 | tf_op jit(solution)/shard_map/pmax | solution.py:33
  245.9 3.5 multiply_convert_fusion
  249.4 5.1 convolution_convert_fusion
  254.6 4.9 convolution_convert_fusion.3
  259.6 21.8 %reduce-scatter.5.cloned.1.call-done = bf16[24,2560]{1,0:T(8,128)(2,1)} async-done(((bf16[384,2560]{1,0:T(8,128)(2,1)}), bf16[24,2560]{1,0:T(8,128)(2,1)}) %reduce-scatter.5.cloned.1.call-update) | async-done | bytes 122896 | tf_op jit(solution)/shard_map/reduce_scatter | solution.py:51
  282.5 131.3 %psum.15 = f32[2560]{0:T(1024)} all-reduce(f32[2560]{0:T(1024)S(1)} %get-tuple-element.5), channel_id=1, replica_groups=mesh['dp'=16,'tensor'=16] {'dp','tensor'}, use_global_device_ids=true, to_apply=%region_11.0 | all-reduce | flops 2560 | bytes 20480 | tf_op jit(solution)/shard_map/psum | solution.py:59
  413.8 1.7 fusion.4
  415.5 330.8 %all-gather.9.cloned.1.call-done = bf16[40960,640]{1,0:T(8,128)(2,1)} async-done(((bf16[2560,640]{1,0:T(8,128)(2,1)}), bf16[40960,640]{1,0:T(8,128)(2,1)}) %all-gather.9.cloned.1.call-update) | async-done | bytes 52428816 | tf_op jit(solution)/shard_map/all_gather | solution.py:67
  746.3 19.8 %reduce_sum.41 = bf16[2560,640]{1,0:T(8,128)(2,1)} reduce(bf16[16,2560,640]{2,1,0:T(8,128)(2,1)} %bitcast.15, bf16[]{:T(256)} %constant.32.clone.1), dimensions={0}, to_apply=%region_8.0 | reduce | flops 24576000 | bytes 55705600 | tf_op jit(solution)/shard_map/reduce_sum | solution.py:67
  766.1 166.3 %all-reduce.2.cloned.1.call-done = bf16[640,2560]{1,0:T(8,128)(2,1)} async-done(((bf16[640,2560]{1,0:T(8,128)(2,1)}), bf16[640,2560]{1,0:T(8,128)(2,1)}) %all-reduce.2.cloned.1.call-update) | async-done | bytes 3276816 | tf_op jit(solution)/shard_map/psum | solution.py:68
  932.4 86.6 %reduce-scatter.3.cloned.1.call-done = bf16[24,2560]{1,0:T(8,128)(2,1)} async-done(((bf16[384,2560]{1,0:T(8,128)(2,1)}), bf16[24,2560]{1,0:T(8,128)(2,1)}) %reduce-scatter.3.cloned.1.call-update) | async-done | bytes 122896 | tf_op jit(solution)/shard_map/reduce_scatter | solution.py:37
  1019.0 3.8 copy.14
  (36 shorter events, 4.9 us)
Async XLA Ops:
  7.2 100.8 %copy-start = (bf16[2560,640]{1,0:T(8,128)(2,1)S(1)}, bf16[2560,640]{1,0:T(8,128)(2,1)}, u32[]{:S(2)}) copy-start(bf16[2560,640]{1,0:T(8,128)(2,1)} %param.7) | copy-start | bytes 9830404
  7.2 100.8 %all-gather.5.cloned.1.call-start = ((), (), s32[]{:S(2)}) async-start(), calls=%async_computation.2 | async-start | bytes 2088960 | tf_op jit(solution)/shard_map/all_gather | solution.py:29
  11.4 8.0 copy-start.2
  11.4 8.0 copy-start.5
  21.9 169.4 %all-gather.7.cloned.1.call-start = ((), (), s32[]{:S(2)}) async-start(), calls=%async_computation.4 | async-start | bytes 2088960 | tf_op jit(solution)/shard_map/all_gather | solution.py:43
  22.7 258.7 %reduce-scatter.5.cloned.1.call-start = ((), (), s32[]{:S(2)}) async-start(), calls=%async_computation.5 | async-start | bytes 2088960 | tf_op jit(solution)/shard_map/reduce_scatter | solution.py:51
  195.8 0.8 copy-start.6
  199.6 546.8 %all-gather.9.cloned.1.call-start = ((), (), s32[]{:S(2)}) async-start(), calls=%async_computation.7 | async-start | bytes 55705600 | tf_op jit(solution)/shard_map/all_gather | solution.py:67
  205.1 39.3 %copy-start.4 = (f32[384,640]{1,0:T(8,128)S(1)}, f32[384,640]{1,0:T(8,128)}, u32[]{:S(2)}) copy-start(f32[384,640]{1,0:T(8,128)} %get-tuple-element.8) | copy-start | bytes 2949124
  205.1 40.8 %copy-start.3 = (f32[384,640]{1,0:T(8,128)S(1)}, f32[384,640]{1,0:T(8,128)}, u32[]{:S(2)}) copy-start(f32[384,640]{1,0:T(8,128)} %get-tuple-element.11) | copy-start | bytes 2949124
  205.1 727.3 %all-reduce.2.cloned.1.call-start = ((), (), s32[]{:S(2)}) async-start(), calls=%async_computation.6 | async-start | bytes 6553600 | tf_op jit(solution)/shard_map/psum | solution.py:68
  254.6 764.4 %reduce-scatter.3.cloned.1.call-start = ((), (), s32[]{:S(2)}) async-start(), calls=%async_computation.3 | async-start | bytes 2088960 | tf_op jit(solution)/shard_map/reduce_scatter | solution.py:37
  746.3 276.5 %copy-start.1 = (bf16[2560,640]{1,0:T(8,128)(2,1)S(1)}, bf16[2560,640]{1,0:T(8,128)(2,1)}, u32[]{:S(2)}) copy-start(bf16[2560,640]{1,0:T(8,128)(2,1)} %param.7) | copy-start | bytes 9830404
Sparse Core Ops, SparseCore 0:
  22.0 85.8 all-gather.4
  109.7 81.4 all-gather.6
  199.7 81.6 reduce-scatter.4
  285.0 461.3 all-gather.8
  749.1 183.2 all-reduce.1
  935.5 83.4 reduce-scatter.2
